TPU v7x, 32 devices: a whole 2x2x4 slice. The times are simulated.
32 devices in a mesh: groups: 2 (over y), dp: 4 (over z), mp: 4 (over x, core).
Axes of the slice: x: 2, y: 2, z: 4, core: 2. Of those that a mesh axis runs over, the one named last changes fastest.
Arguments:
- queries: bfloat16 [4, 192, 8192], P(None, ('groups', 'dp'), 'mp'), parts along dimension 1, may hold values from -120 to 120
- new_keys: bfloat16 [4, 192, 1024], P(None, ('groups', 'dp'), 'mp'), parts along dimension 1, may hold values from -4 to 4
- new_values: bfloat16 [4, 192, 1024], P(None, ('groups', 'dp'), 'mp'), parts along dimension 1, may hold values from -4 to 4
- key_cache: bfloat16 [192, 128, 1024], P(('groups', 'dp'), None, 'mp'), parts along dimension 0, may hold values from -5 to 5
- value_cache: bfloat16 [192, 128, 1024], P(('groups', 'dp'), None, 'mp'), parts along dimension 0, may hold values from -4 to 4
- lengths: int32 [192], P('groups'), parts along dimension 0, may hold values from 8 to 124, as said below
- migrations: int32 [16, 3], P('groups'), parts along dimension 0, may hold values from 0 to 95, as said below
- receive_counts: int32 [8], P('groups'), parts along dimension 0, may hold values from 1 to 3, as said below
Outputs:
- attention: bfloat16 [4, 192, 8192], P(None, ('groups', 'dp'), 'mp'), parts along dimension 1
- landed_keys: bfloat16 [24, 128, 1024], P(('groups', 'dp'), None, 'mp'), parts along dimension 0
- landed_values: bfloat16 [24, 128, 1024], P(('groups', 'dp'), None, 'mp'), parts along dimension 0
There are 2 independent parts, one for each index of `groups`. A program takes and returns all parts, laid end to end along the dimension named above; each array names one. Nothing has to cross between parts.
Inputs may be any that keep to these rules, and one draw needn't show every extreme that they name: `lengths`: rows named in migrations hold 64 to 124 cached positions, all other rows 8 to 32; some row holds exactly 124. `migrations`: entries come in order of source, 2 for every source; an entry's row lies among the source's rows (row // 24 equals source); the 2 destinations of one source differ from each other and from the source; every index of dp receives 2 - 1 to 3 rows, and some receive 3. receive_counts[d] is the number of entries of migrations whose destination is d.
All inputs are finite; a program needn't handle non-finite values.
Results may differ from a plain program's by a relative error of at most 0.0049.
Values may be sent and summed in bfloat16 or wider, within the bound.
A program may use at most 64 MiB of HBM per device.

v0:
```python
import jax
import jax.numpy as jnp
from jax import lax
from jax.sharding import PartitionSpec as P

HEAD_DIM = 128


masked_score = -1e30


def extend_cache(cache_rows, fresh, row_lengths):
    positions = jnp.arange(cache_rows.shape[1], dtype=jnp.int32)[None, :, None]
    limits = row_lengths[:, None, None]
    result = jnp.where(positions < limits, cache_rows, jnp.zeros((), cache_rows.dtype))
    for offset in range(fresh.shape[0]):
        result = jnp.where(positions == limits + offset, fresh[offset][:, None, :], result)
    return result


def attend_rows(queries, key_rows, value_rows, row_lengths):
    step_count, row_count, query_width = queries.shape
    capacity, kv_width = (key_rows.shape[1], key_rows.shape[2])
    kv_local = kv_width // HEAD_DIM
    per_group = query_width // kv_width
    query_view = queries.reshape(step_count, row_count, kv_local, per_group, HEAD_DIM)
    key_view = key_rows.reshape(row_count, capacity, kv_local, HEAD_DIM)
    value_view = value_rows.reshape(row_count, capacity, kv_local, HEAD_DIM)
    scores = jnp.einsum(
        "srkgd,rpkd->rkgsp", query_view, key_view, preferred_element_type=jnp.float32
    ) * HEAD_DIM ** (-0.5)
    positions = jnp.arange(capacity, dtype=jnp.int32)[None, None, :]
    allowed = (
        positions
        <= row_lengths[:, None, None] + jnp.arange(step_count, dtype=jnp.int32)[None, :, None]
    )
    scores = jnp.where(allowed[:, None, None], scores, masked_score)
    highest = jnp.max(scores, axis=-1, keepdims=True)
    exponent = jnp.exp(scores - highest)
    weights = (exponent / jnp.sum(exponent, axis=-1, keepdims=True)).astype(jnp.bfloat16)
    result = jnp.einsum(
        "rkgsp,rpkd->srkgd", weights, value_view, preferred_element_type=jnp.float32
    )
    return result.reshape(step_count, row_count, query_width).astype(jnp.bfloat16)


def on_device(
    queries, new_keys, new_values, key_cache, value_cache, lengths, migrations, receive_counts
):
    own_index = lax.axis_index("dp")
    peer_count = lax.axis_size("dp")
    rows_dev = key_cache.shape[0]
    leave_count = migrations.shape[0] // peer_count
    land_count = leave_count + 1
    peer_ids = jnp.arange(peer_count, dtype=jnp.int32)
    local_slot = jnp.arange(rows_dev, dtype=jnp.int32)
    zero_value = jnp.zeros((), jnp.bfloat16)
    dest_table = migrations[:, 2].reshape(peer_count, leave_count)
    row_table = migrations[:, 0].reshape(peer_count, leave_count)
    own_dests = lax.dynamic_index_in_dim(dest_table, own_index, 0, keepdims=False)
    own_slots = (
        lax.dynamic_index_in_dim(row_table, own_index, 0, keepdims=False) - own_index * rows_dev
    )
    own_lengths = lax.dynamic_slice_in_dim(lengths, own_index * rows_dev, rows_dev)
    to_peer = own_dests[None, :] == peer_ids[:, None]
    send_valid = jnp.any(to_peer, axis=1)
    send_slot = jnp.sum(jnp.where(to_peer, own_slots[None, :], 0), axis=1)
    toward_me = dest_table == own_index
    from_source = jnp.any(toward_me, axis=1)
    incoming_row = jnp.sum(jnp.where(toward_me, row_table, 0), axis=1)
    source_flags = from_source.astype(jnp.int32)
    slot_of = jnp.cumsum(source_flags) - source_flags
    landing_ids = jnp.arange(land_count, dtype=jnp.int32)
    landing_pick = from_source[None, :] & (slot_of[None, :] == landing_ids[:, None])
    land_valid = jnp.any(landing_pick, axis=1) & (landing_ids < receive_counts[own_index])
    land_source = jnp.sum(jnp.where(landing_pick, peer_ids[None, :], 0), axis=1)

    def rows_out(table, axis_pos):
        picked = jnp.take(table, send_slot, axis=axis_pos, mode="clip")
        if axis_pos == 0:
            return jnp.where(send_valid[:, None, None], picked, zero_value)
        return jnp.transpose(jnp.where(send_valid[None, :, None], picked, zero_value), (1, 0, 2))

    arrived = (
        lax.all_to_all(rows_out(key_cache, 0), "dp", split_axis=0, concat_axis=0, tiled=True),
        lax.all_to_all(rows_out(value_cache, 0), "dp", split_axis=0, concat_axis=0, tiled=True),
        lax.all_to_all(rows_out(queries, 1), "dp", split_axis=0, concat_axis=0, tiled=True),
        lax.all_to_all(rows_out(new_keys, 1), "dp", split_axis=0, concat_axis=0, tiled=True),
        lax.all_to_all(rows_out(new_values, 1), "dp", split_axis=0, concat_axis=0, tiled=True),
    )

    def rows_in(table, turned):
        picked = jnp.where(
            land_valid[:, None, None], jnp.take(table, land_source, axis=0, mode="clip"), zero_value
        )
        if turned:
            return jnp.transpose(picked, (1, 0, 2))
        return picked

    land_rows = jnp.take(incoming_row, land_source, axis=0, mode="clip")
    land_lengths = jnp.where(land_valid, jnp.take(lengths, land_rows, axis=0, mode="clip"), 0)
    landed_keys = extend_cache(rows_in(arrived[0], False), rows_in(arrived[3], True), land_lengths)
    landed_values = extend_cache(
        rows_in(arrived[1], False), rows_in(arrived[4], True), land_lengths
    )
    landed_out = attend_rows(rows_in(arrived[2], True), landed_keys, landed_values, land_lengths)
    back_slots = jnp.minimum(slot_of, land_count - 1)
    going_back = jnp.where(
        from_source[None, :, None],
        jnp.take(landed_out, back_slots, axis=1, mode="clip"),
        zero_value,
    )
    returned = lax.all_to_all(
        jnp.transpose(going_back, (1, 0, 2)), "dp", split_axis=0, concat_axis=0, tiled=True
    )
    leaving_match = own_slots[None, :] == local_slot[:, None]
    leaving = jnp.any(leaving_match, axis=1)
    keep_flags = 1 - leaving.astype(jnp.int32)
    stay_rank = jnp.cumsum(keep_flags) - keep_flags
    stay_count = rows_dev - leave_count
    stay_pick = (keep_flags[None, :] == 1) & (
        stay_rank[None, :] == jnp.arange(stay_count, dtype=jnp.int32)[:, None]
    )
    stay_index = jnp.sum(jnp.where(stay_pick, local_slot[None, :], 0), axis=1)
    stay_lengths = jnp.take(own_lengths, stay_index, axis=0, mode="clip")
    stay_keys = extend_cache(
        jnp.take(key_cache, stay_index, axis=0, mode="clip"),
        jnp.take(new_keys, stay_index, axis=1, mode="clip"),
        stay_lengths,
    )
    stay_values = extend_cache(
        jnp.take(value_cache, stay_index, axis=0, mode="clip"),
        jnp.take(new_values, stay_index, axis=1, mode="clip"),
        stay_lengths,
    )
    stay_out = attend_rows(
        jnp.take(queries, stay_index, axis=1, mode="clip"), stay_keys, stay_values, stay_lengths
    )
    dest_of_row = jnp.sum(jnp.where(leaving_match, own_dests[None, :], 0), axis=1)
    from_back = jnp.transpose(jnp.take(returned, dest_of_row, axis=0, mode="clip"), (1, 0, 2))
    from_stay = jnp.take(stay_out, jnp.clip(stay_rank, 0, stay_count - 1), axis=1, mode="clip")
    attention = jnp.where(leaving[None, :, None], from_back, from_stay)
    return (attention, landed_keys, landed_values)


def solution(mesh):
    placed = (
        P(None, ("groups", "dp"), "mp"),
        P(None, ("groups", "dp"), "mp"),
        P(None, ("groups", "dp"), "mp"),
        P(("groups", "dp"), None, "mp"),
        P(("groups", "dp"), None, "mp"),
        P("groups"),
        P("groups", None),
        P("groups"),
    )
    return jax.shard_map(
        on_device,
        mesh=mesh,
        in_specs=placed,
        out_specs=(
            P(None, ("groups", "dp"), "mp"),
            P(("groups", "dp"), None, "mp"),
            P(("groups", "dp"), None, "mp"),
        ),
        check_vma=False,
    )
```

profile of v0, /device:TPU:0, one launch (start us, length us, event | category | flops | bytes accessed | tf_op | source)
XLA Modules:
  0.0 110.3 jit_solution(11848961115161490339)
XLA Ops:
  0.7 0.9 slice_reduce_fusion
  2.3 1.4 %gather_fusion.2 = bf16[4,4,256]{2,0,1:T(4,128)(2,1)S(1)} fusion(bf16[4,24,256]{2,1,0:T(8,128)(2,1)} %param.10, s32[1024]{0:T(1024)S(1)} %pad_clamp_fusion.4), kind=kCustom, calls=%fused_computation.2 | custom fusion | bytes 16400 | tf_op jit(solution)/shard_map/jit(_take)/gather | solution.py:79
  3.7 1.4 %gather_fusion.6 = bf16[4,4,256]{2,0,1:T(4,128)(2,1)S(1)} fusion(bf16[4,24,256]{2,1,0:T(8,128)(2,1)} %param.9, s32[1024]{0:T(1024)S(1)} %pad_clamp_fusion.4), kind=kCustom, calls=%fused_computation.6 | custom fusion | bytes 16400 | tf_op jit(solution)/shard_map/jit(_take)/gather | solution.py:79
  5.1 0.6 copy.70
  5.7 6.3 %all-to-all-start = ((bf16[4,4,256]{2,1,0:T(4,128)(2,1)}), bf16[4,4,256]{2,1,0:T(4,128)(2,1)}, u32[]{:S(2)}, u32[]{:S(2)}) async-start(bf16[4,4,256]{2,1,0:T(4,128)(2,1)} %copy.70), calls=%async_computation | async-start | bytes 16384 | tf_op jit(solution)/shard_map/all_to_all | solution.py:89
  12.3 0.7 clamp_reduce_fusion
  13.1 0.7 dynamic_slice.16
  13.9 0.7 gather_fusion.14
  14.6 0.6 broadcast_add_fusion.2
  15.2 0.7 iota_compare_fusion.2
  15.8 0.7 iota_add_fusion
  16.5 2.2 %gather_fusion.17 = bf16[22,4,256]{2,0,1:T(8,128)(2,1)} fusion(bf16[4,24,256]{2,1,0:T(8,128)(2,1)} %param.9, s32[1024]{0:T(1024)S(1)} %pad_clamp_fusion.1), kind=kCustom, calls=%fused_computation.17 | custom fusion | bytes 90200 | tf_op jit(solution)/shard_map/jit(_take)/gather | solution.py:128
  18.7 1.4 %gather_fusion.15 = bf16[22,4,256]{2,0,1:T(8,128)(2,1)} fusion(bf16[4,24,256]{2,1,0:T(8,128)(2,1)S(1)} %copy-done.3, s32[1024]{0:T(1024)S(1)} %pad_clamp_fusion.1), kind=kCustom, calls=%fused_computation.15 | custom fusion | bytes 90200 | tf_op jit(solution)/shard_map/jit(_take)/gather | solution.py:133
  20.1 1.9 %gather_fusion.19 = bf16[22,4,2048]{2,0,1:T(8,128)(2,1)S(1)} fusion(bf16[4,24,2048]{2,1,0:T(8,128)(2,1)S(1)} %copy-done.2, s32[1024]{0:T(1024)S(1)} %pad_clamp_fusion.1), kind=kCustom, calls=%fused_computation.19 | custom fusion | bytes 720984 | tf_op jit(solution)/shard_map/jit(_take)/gather | solution.py:137
  22.0 1.5 %gather_fusion.10 = bf16[4,4,2048]{2,0,1:T(4,128)(2,1)} fusion(bf16[4,24,2048]{2,1,0:T(8,128)(2,1)S(1)} %copy-done.2, s32[1024]{0:T(1024)S(1)} %pad_clamp_fusion.4), kind=kCustom, calls=%fused_computation.10 | custom fusion | bytes 131088 | tf_op jit(solution)/shard_map/jit(_take)/gather | solution.py:79
  23.9 0.7 select_reduce_fusion.2
  24.6 0.6 fusion.103
  25.2 2.1 %gather_fusion.16 = bf16[22,128,256]{2,1,0:T(8,128)(2,1)} fusion(bf16[24,128,256]{2,1,0:T(8,128)(2,1)S(1)} %copy-done, s32[1024]{0:T(1024)} %copy-done.12), kind=kCustom, calls=%fused_computation.16 | custom fusion | bytes 2883672 | tf_op jit(solution)/shard_map/jit(_take)/gather | solution.py:132
  27.3 1.4 %gather_fusion.4 = bf16[4,128,256]{2,1,0:T(8,128)(2,1)} fusion(bf16[24,128,256]{2,1,0:T(8,128)(2,1)S(1)} %copy-done, s32[1024]{0:T(1024)} %copy-done.13), kind=kCustom, calls=%fused_computation.4 | custom fusion | bytes 524304 | tf_op jit(solution)/shard_map/jit(_take)/gather | solution.py:79
  28.7 2.1 %gather_fusion.18 = bf16[22,128,256]{2,1,0:T(8,128)(2,1)} fusion(bf16[24,128,256]{2,1,0:T(8,128)(2,1)S(1)} %copy-done.4, s32[1024]{0:T(1024)} %copy-done.12), kind=kCustom, calls=%fused_computation.18 | custom fusion | bytes 2883672 | tf_op jit(solution)/shard_map/jit(_take)/gather | solution.py:127
  30.8 1.4 %gather_fusion.8 = bf16[4,128,256]{2,1,0:T(8,128)(2,1)} fusion(bf16[24,128,256]{2,1,0:T(8,128)(2,1)S(1)} %copy-done.4, s32[1024]{0:T(1024)} %copy-done.13), kind=kCustom, calls=%fused_computation.8 | custom fusion | bytes 524304 | tf_op jit(solution)/shard_map/jit(_take)/gather | solution.py:79
  32.2 0.7 pad_clamp_fusion.6
  32.9 0.6 gather_fusion
  33.6 0.6 gather_fusion.1
  34.2 1.3 %dynamic_slice.14 = s32[1]{0:T(128)} dynamic-slice(s32[4]{0:T(128)} %param.15, s32[]{:T(128)S(6)} %select_n.239), dynamic_slice_sizes={1} | dynamic-slice | bytes 12 | tf_op jit(solution)/shard_map/dynamic_slice | solution.py:75
  35.5 1.8 %broadcast_add_fusion.5 = (s32[3]{0:T(128)S(1)}, s32[3]{0:T(128)S(1)}, pred[3]{0:T(512)(128)(4,1)}) fusion(s32[3]{0:T(128)S(1)} %gather_fusion.1, pred[3]{0:T(512)(128)(4,1)} %fusion.103, s32[]{:T(128)} %bitcast.3), kind=kLoop, calls=%fused_computation.187 | loop fusion | flops 12 | bytes 46 | tf_op jit(solution)/shard_map/add | solution.py:17
  37.3 0.6 iota_compare_fusion.9
  38.0 1.2 %minimum_bitcast_fusion = s32[4]{0:T(128)} fusion(s32[4,1]{0,1:T(1,128)} %copy-done.35, pred[4]{0:T(512)(128)(4,1)} %copy-done.27), kind=kLoop, calls=%fused_computation.176 | loop fusion | flops 12 | bytes 36 | tf_op jit(solution)/shard_map/min | solution.py:107
  39.2 1.3 %select_reduce_fusion.4 = s32[24]{0:T(128)} fusion(s32[2]{0:T(128)} %copy-done.33, s32[2]{0:T(128)} %copy-done.34), kind=kLoop, calls=%fused_computation.169 | loop fusion | flops 120 | bytes 112 | tf_op jit(solution)/shard_map/reduce_sum | solution.py:139
  40.5 0.7 iota_compare_fusion.3
  41.3 0.7 iota_compare_fusion.4
  41.9 0.7 iota_compare_fusion.6
  42.6 0.8 iota_compare_fusion
  43.4 0.8 fusion.111
  44.3 1.0 reshape.689
  45.8 0.9 broadcast_select_fusion
  46.7 5.2 %fusion.114 = (f32[22,2,8,4]{2,3,1,0:T(4,128)}, f32[22,2,8,4,128]{4,2,3,1,0:T(8,128)}) fusion(pred[22,128]{1,0:T(8,128)(4,1)S(1)} %copy-done.22, pred[22,128]{1,0:T(8,128)(4,1)S(1)} %copy-done.20, pred[22,128]{1,0:T(8,128)(4,1)S(1)} %iota_compare_fusion.3, pred[22,128]{1,0:T(8,128)(4,1)S(1)} %iota_compare_fusion.4, ...), kind=kOutput, calls=%fused_computation.206 | convolution fusion | flops 50462848 | bytes 2599168 | tf_op jit(solution)/shard_map/sub | solution.py:39
  52.0 3.5 %fusion.40 = bf16[4,22,2,8,128]{4,3,0,2,1:T(8,128)(2,1)S(1)} fusion(pred[22,128]{1,0:T(8,128)(4,1)S(1)} %copy-done.23, pred[22,128]{1,0:T(8,128)(4,1)S(1)} %copy-done.21, pred[22,128]{1,0:T(8,128)(4,1)} %copy-done.17, pred[22,128]{1,0:T(8,128)(4,1)} %copy-done.18, pred[22,128]{1,0:T(8,128)(4,1)} %copy-done.19, ...), kind=kOutput, calls=%fused_computation.53 | convolution fusion | flops 50282496 | bytes 2587904 | tf_op jit(solution)/shard_map/rkgsp,rpkd->srkgd/dot_general | solution.py:41
  55.5 0.6 copy.72
  56.1 5.1 %all-to-all-start.2 = ((bf16[4,4,256]{2,1,0:T(4,128)(2,1)}), bf16[4,4,256]{2,1,0:T(4,128)(2,1)S(1)}, u32[]{:S(2)}, u32[]{:S(2)}) async-start(bf16[4,4,256]{2,1,0:T(4,128)(2,1)} %copy.72), calls=%async_computation.2 | async-start | bytes 16384 | tf_op jit(solution)/shard_map/all_to_all | solution.py:88
  61.4 0.7 copy.74
  62.0 0.9 gather_fusion.20
  62.9 1.3 %gather_fusion.3 = bf16[3,4,256]{2,1,0:T(4,128)(2,1)S(1)} fusion(bf16[4,4,256]{2,1,0:T(4,128)(2,1)} %all-to-all-done, s32[1024]{0:T(1024)S(1)} %copy-done.11), kind=kCustom, calls=%fused_computation.3 | custom fusion | bytes 12300 | tf_op jit(solution)/shard_map/jit(_take)/gather | solution.py:94
  64.2 2.6 %all-to-all-done.2 = bf16[4,4,256]{2,1,0:T(4,128)(2,1)S(1)} async-done(((bf16[4,4,256]{2,1,0:T(4,128)(2,1)}), bf16[4,4,256]{2,1,0:T(4,128)(2,1)S(1)}, u32[]{:S(2)}, u32[]{:S(2)}) %all-to-all-start.2) | async-done | bytes 8224 | tf_op jit(solution)/shard_map/all_to_all | solution.py:88
  66.8 3.3 %all-to-all-start.4 = ((bf16[4,4,2048]{2,1,0:T(4,128)(2,1)}), bf16[4,4,2048]{2,1,0:T(4,128)(2,1)S(1)}, u32[]{:S(2)}, u32[]{:S(2)}) async-start(bf16[4,4,2048]{2,1,0:T(4,128)(2,1)} %copy.74), calls=%async_computation.4 | async-start | bytes 131072 | tf_op jit(solution)/shard_map/all_to_all | solution.py:87
  70.1 0.6 gather_fusion.7
  70.7 5.1 %all-to-all-done.4 = bf16[4,4,2048]{2,1,0:T(4,128)(2,1)S(1)} async-done(((bf16[4,4,2048]{2,1,0:T(4,128)(2,1)}), bf16[4,4,2048]{2,1,0:T(4,128)(2,1)S(1)}, u32[]{:S(2)}, u32[]{:S(2)}) %all-to-all-start.4) | async-done | bytes 65568 | tf_op jit(solution)/shard_map/all_to_all | solution.py:87
  75.8 3.4 %all-to-all-start.3 = ((bf16[4,128,256]{2,1,0:T(8,128)(2,1)}), bf16[4,128,256]{2,1,0:T(8,128)(2,1)S(1)}, u32[]{:S(2)}, u32[]{:S(2)}) async-start(bf16[4,128,256]{2,1,0:T(8,128)(2,1)} %get-tuple-element.59), calls=%async_computation.3 | async-start | bytes 524288 | tf_op jit(solution)/shard_map/all_to_all | solution.py:85
  79.5 0.6 gather_fusion.11
  80.1 5.8 %all-to-all-done.3 = bf16[4,128,256]{2,1,0:T(8,128)(2,1)S(1)} async-done(((bf16[4,128,256]{2,1,0:T(8,128)(2,1)}), bf16[4,128,256]{2,1,0:T(8,128)(2,1)S(1)}, u32[]{:S(2)}, u32[]{:S(2)}) %all-to-all-start.3) | async-done | bytes 262176 | tf_op jit(solution)/shard_map/all_to_all | solution.py:85
  85.9 3.4 %all-to-all-start.1 = ((bf16[4,128,256]{2,1,0:T(8,128)(2,1)}), bf16[4,128,256]{2,1,0:T(8,128)(2,1)S(1)}, u32[]{:S(2)}, u32[]{:S(2)}) async-start(bf16[4,128,256]{2,1,0:T(8,128)(2,1)} %get-tuple-element.60), calls=%async_computation.1 | async-start | bytes 524288 | tf_op jit(solution)/shard_map/all_to_all | solution.py:86
  89.5 0.6 gather_fusion.9
  90.1 0.9 fusion.46
  91.2 5.0 %all-to-all-done.1 = bf16[4,128,256]{2,1,0:T(8,128)(2,1)S(1)} async-done(((bf16[4,128,256]{2,1,0:T(8,128)(2,1)}), bf16[4,128,256]{2,1,0:T(8,128)(2,1)S(1)}, u32[]{:S(2)}, u32[]{:S(2)}) %all-to-all-start.1) | async-done | bytes 262176 | tf_op jit(solution)/shard_map/all_to_all | solution.py:86
  96.1 0.6 gather_fusion.5
  96.7 0.7 fusion.47
  97.5 0.6 gather_fusion.12
  98.2 0.7 copy.78
  98.9 3.4 %all-to-all-start.5 = ((bf16[4,4,2048]{2,1,0:T(4,128)(2,1)}), bf16[4,4,2048]{2,1,0:T(4,128)(2,1)S(1)}, u32[]{:S(2)}, u32[]{:S(2)}) async-start(bf16[4,4,2048]{2,1,0:T(4,128)(2,1)} %copy.78), calls=%async_computation.5 | async-start | bytes 131072 | tf_op jit(solution)/shard_map/all_to_all | solution.py:113
  102.3 1.1 select_select_fusion
  103.4 4.7 %all-to-all-done.5 = bf16[4,4,2048]{2,1,0:T(4,128)(2,1)S(1)} async-done(((bf16[4,4,2048]{2,1,0:T(4,128)(2,1)}), bf16[4,4,2048]{2,1,0:T(4,128)(2,1)S(1)}, u32[]{:S(2)}, u32[]{:S(2)}) %all-to-all-start.5) | async-done | bytes 65568 | tf_op jit(solution)/shard_map/all_to_all | solution.py:113
  108.1 0.9 gather_fusion.13
  109.0 0.3 select_bitcast_fusion
  109.3 1.0 copy.86
  (139 shorter events, 3.2 us)
Async XLA Ops:
  0.6 24.6 %copy-start = (bf16[24,128,256]{2,1,0:T(8,128)(2,1)S(1)}, bf16[24,128,256]{2,1,0:T(8,128)(2,1)}, u32[]{:S(2)}) copy-start(bf16[24,128,256]{2,1,0:T(8,128)(2,1)} %param.12) | copy-start | bytes 4718596
  0.6 18.1 %copy-start.3 = (bf16[4,24,256]{2,1,0:T(8,128)(2,1)S(1)}, bf16[4,24,256]{2,1,0:T(8,128)(2,1)}, u32[]{:S(2)}) copy-start(bf16[4,24,256]{2,1,0:T(8,128)(2,1)} %param.10) | copy-start | bytes 147460
  0.7 19.4 %copy-start.2 = (bf16[4,24,2048]{2,1,0:T(8,128)(2,1)S(1)}, bf16[4,24,2048]{2,1,0:T(8,128)(2,1)}, u32[]{:S(2)}) copy-start(bf16[4,24,2048]{2,1,0:T(8,128)(2,1)} %param.8) | copy-start | bytes 1179652
  1.7 0.5 copy-start.33
  1.7 10.5 %copy-start.34 = (s32[2]{0:T(128)}, s32[2]{0:T(128)S(1)}, u32[]{:S(2)}) copy-start(s32[2]{0:T(128)S(1)} %get-tuple-element.68) | copy-start | bytes 28
  1.8 11.3 %copy-start.15 = (pred[4]{0:T(512)(128)(4,1)}, pred[4]{0:T(512)(128)(4,1)S(1)}, u32[]{:S(2)}) copy-start(pred[4]{0:T(512)(128)(4,1)S(1)} %fusion.101) | copy-start | bytes 16
  2.3 19.8 %copy-start.13 = (s32[1024]{0:T(1024)}, s32[1024]{0:T(1024)S(1)}, u32[]{:S(2)}) copy-start(s32[1024]{0:T(1024)S(1)} %pad_clamp_fusion.4) | copy-start | bytes 12292
  5.7 50.4 %all-to-all-start = ((bf16[4,4,256]{2,1,0:T(4,128)(2,1)}), bf16[4,4,256]{2,1,0:T(4,128)(2,1)}, u32[]{:S(2)}, u32[]{:S(2)}) async-start(bf16[4,4,256]{2,1,0:T(4,128)(2,1)} %copy.70), calls=%async_computation | async-start | bytes 16384 | tf_op jit(solution)/shard_map/all_to_all | solution.py:89
  12.1 9.9 %copy-start.25 = (pred[24]{0:T(512)(128)(4,1)}, pred[24]{0:T(512)(128)(4,1)S(1)}, u32[]{:S(2)}) copy-start(pred[24]{0:T(512)(128)(4,1)S(1)} %fusion.104) | copy-start | bytes 76
  13.1 8.9 %copy-start.12 = (s32[1024]{0:T(1024)}, s32[1024]{0:T(1024)S(1)}, u32[]{:S(2)}) copy-start(s32[1024]{0:T(1024)S(1)} %pad_clamp_fusion.1) | copy-start | bytes 12292
  23.7 3.6 %copy-start.27 = (pred[4]{0:T(512)(128)(4,1)}, pred[4]{0:T(512)(128)(4,1)S(1)}, u32[]{:S(2)}) copy-start(pred[4]{0:T(512)(128)(4,1)S(1)} %reduce_or.37) | copy-start | bytes 16
  23.9 0.7 copy-start.35
  25.2 3.5 %copy-start.4 = (bf16[24,128,256]{2,1,0:T(8,128)(2,1)S(1)}, bf16[24,128,256]{2,1,0:T(8,128)(2,1)}, u32[]{:S(2)}) copy-start(bf16[24,128,256]{2,1,0:T(8,128)(2,1)} %param.11) | copy-start | bytes 4718596
  28.7 4.8 %copy-start.1 = (s32[96]{0:T(128)S(1)}, s32[96]{0:T(128)}, u32[]{:S(2)}) copy-start(s32[96]{0:T(128)} %param.13) | copy-start | bytes 1156
  32.2 13.1 %copy-start.9 = (bf16[22,4,256]{2,0,1:T(8,128)(2,1)S(1)}, bf16[22,4,256]{2,0,1:T(8,128)(2,1)}, u32[]{:S(2)}) copy-start(bf16[22,4,256]{2,0,1:T(8,128)(2,1)} %gather_fusion.15) | copy-start | bytes 135172
  32.2 13.2 %copy-start.24 = (s32[24]{0:T(128)S(1)}, s32[24]{0:T(128)}, u32[]{:S(2)}) copy-start(s32[24]{0:T(128)} %get-tuple-element.15) | copy-start | bytes 292
  32.2 13.2 %copy-start.8 = (bf16[4,4,2048]{2,0,1:T(4,128)(2,1)S(1)}, bf16[4,4,2048]{2,0,1:T(4,128)(2,1)}, u32[]{:S(2)}) copy-start(bf16[4,4,2048]{2,0,1:T(4,128)(2,1)} %gather_fusion.10) | copy-start | bytes 196612
  32.2 13.2 %copy-start.16 = (pred[4]{0:T(512)(128)(4,1)S(1)}, pred[4]{0:T(512)(128)(4,1)}, u32[]{:S(2)}) copy-start(pred[4]{0:T(512)(128)(4,1)} %copy-done.15) | copy-start | bytes 16
  32.2 13.6 %copy-start.6 = (bf16[4,128,256]{2,1,0:T(8,128)(2,1)S(1)}, bf16[4,128,256]{2,1,0:T(8,128)(2,1)}, u32[]{:S(2)}) copy-start(bf16[4,128,256]{2,1,0:T(8,128)(2,1)} %gather_fusion.4) | copy-start | bytes 786436
  32.2 13.6 %copy-start.7 = (bf16[4,128,256]{2,1,0:T(8,128)(2,1)S(1)}, bf16[4,128,256]{2,1,0:T(8,128)(2,1)}, u32[]{:S(2)}) copy-start(bf16[4,128,256]{2,1,0:T(8,128)(2,1)} %gather_fusion.8) | copy-start | bytes 786436
  32.9 10.5 %copy-start.10 = (s32[1024]{0:T(1024)}, s32[1024]{0:T(1024)S(1)}, u32[]{:S(2)}) copy-start(s32[1024]{0:T(1024)S(1)} %pad_clamp_fusion.6) | copy-start | bytes 12292
  33.6 13.1 %copy-start.20 = (pred[22,128]{1,0:T(8,128)(4,1)S(1)}, pred[22,128]{1,0:T(8,128)(4,1)}, u32[]{:S(2)}) copy-start(pred[22,128]{1,0:T(8,128)(4,1)} %get-tuple-element.53) | copy-start | bytes 8452
  33.6 13.1 %copy-start.22 = (pred[22,128]{1,0:T(8,128)(4,1)S(1)}, pred[22,128]{1,0:T(8,128)(4,1)}, u32[]{:S(2)}) copy-start(pred[22,128]{1,0:T(8,128)(4,1)} %get-tuple-element.54) | copy-start | bytes 8452
  41.3 10.7 %copy-start.17 = (pred[22,128]{1,0:T(8,128)(4,1)}, pred[22,128]{1,0:T(8,128)(4,1)S(1)}, u32[]{:S(2)}) copy-start(pred[22,128]{1,0:T(8,128)(4,1)S(1)} %iota_compare_fusion.3) | copy-start | bytes 8452
  41.9 10.0 %copy-start.18 = (pred[22,128]{1,0:T(8,128)(4,1)}, pred[22,128]{1,0:T(8,128)(4,1)S(1)}, u32[]{:S(2)}) copy-start(pred[22,128]{1,0:T(8,128)(4,1)S(1)} %iota_compare_fusion.4) | copy-start | bytes 8452
  42.6 9.3 %copy-start.19 = (pred[22,128]{1,0:T(8,128)(4,1)}, pred[22,128]{1,0:T(8,128)(4,1)S(1)}, u32[]{:S(2)}) copy-start(pred[22,128]{1,0:T(8,128)(4,1)S(1)} %iota_compare_fusion.6) | copy-start | bytes 8452
  46.7 5.2 %copy-start.5 = (bf16[22,128,256]{2,1,0:T(8,128)(2,1)S(1)}, bf16[22,128,256]{2,1,0:T(8,128)(2,1)}, u32[]{:S(2)}) copy-start(bf16[22,128,256]{2,1,0:T(8,128)(2,1)} %gather_fusion.16) | copy-start | bytes 4325380
  46.7 5.2 %copy-start.21 = (pred[22,128]{1,0:T(8,128)(4,1)S(1)}, pred[22,128]{1,0:T(8,128)(4,1)}, u32[]{:S(2)}) copy-start(pred[22,128]{1,0:T(8,128)(4,1)} %get-tuple-element.53) | copy-start | bytes 8452
  46.7 5.2 %copy-start.23 = (pred[22,128]{1,0:T(8,128)(4,1)S(1)}, pred[22,128]{1,0:T(8,128)(4,1)}, u32[]{:S(2)}) copy-start(pred[22,128]{1,0:T(8,128)(4,1)} %get-tuple-element.54) | copy-start | bytes 8452
  51.9 3.5 %copy-start.32 = (s32[4]{0:T(128)S(1)}, s32[4]{0:T(128)}, u32[]{:S(2)}) copy-start(s32[4]{0:T(128)} %minimum_bitcast_fusion) | copy-start | bytes 52
  52.0 9.2 %copy-start.31 = (s32[24]{0:T(128)S(1)}, s32[24]{0:T(128)}, u32[]{:S(2)}) copy-start(s32[24]{0:T(128)} %select_reduce_fusion.4) | copy-start | bytes 292
  55.4 7.5 %copy-start.11 = (s32[1024]{0:T(1024)S(1)}, s32[1024]{0:T(1024)}, u32[]{:S(2)}) copy-start(s32[1024]{0:T(1024)} %copy-done.10) | copy-start | bytes 12292
  55.5 15.2 %copy-start.14 = (pred[3]{0:T(512)(128)(4,1)S(1)}, pred[3]{0:T(512)(128)(4,1)}, u32[]{:S(2)}) copy-start(pred[3]{0:T(512)(128)(4,1)} %get-tuple-element.29) | copy-start | bytes 13
  56.1 10.7 %all-to-all-start.2 = ((bf16[4,4,256]{2,1,0:T(4,128)(2,1)}), bf16[4,4,256]{2,1,0:T(4,128)(2,1)S(1)}, u32[]{:S(2)}, u32[]{:S(2)}) async-start(bf16[4,4,256]{2,1,0:T(4,128)(2,1)} %copy.72), calls=%async_computation.2 | async-start | bytes 16384 | tf_op jit(solution)/shard_map/all_to_all | solution.py:88
  62.0 28.0 %copy-start.29 = (pred[3,128]{1,0:T(4,128)(4,1)S(1)}, pred[3,128]{1,0:T(4,128)(4,1)}, u32[]{:S(2)}) copy-start(pred[3,128]{1,0:T(4,128)(4,1)} %get-tuple-element.63) | copy-start | bytes 1156
  62.0 28.0 %copy-start.30 = (pred[3,128]{1,0:T(4,128)(4,1)S(1)}, pred[3,128]{1,0:T(4,128)(4,1)}, u32[]{:S(2)}) copy-start(pred[3,128]{1,0:T(4,128)(4,1)} %get-tuple-element.64) | copy-start | bytes 1156
  66.8 9.0 %all-to-all-start.4 = ((bf16[4,4,2048]{2,1,0:T(4,128)(2,1)}), bf16[4,4,2048]{2,1,0:T(4,128)(2,1)S(1)}, u32[]{:S(2)}, u32[]{:S(2)}) async-start(bf16[4,4,2048]{2,1,0:T(4,128)(2,1)} %copy.74), calls=%async_computation.4 | async-start | bytes 131072 | tf_op jit(solution)/shard_map/all_to_all | solution.py:87
  75.8 10.2 %all-to-all-start.3 = ((bf16[4,128,256]{2,1,0:T(8,128)(2,1)}), bf16[4,128,256]{2,1,0:T(8,128)(2,1)S(1)}, u32[]{:S(2)}, u32[]{:S(2)}) async-start(bf16[4,128,256]{2,1,0:T(8,128)(2,1)} %get-tuple-element.59), calls=%async_computation.3 | async-start | bytes 524288 | tf_op jit(solution)/shard_map/all_to_all | solution.py:85
  85.9 10.2 %all-to-all-start.1 = ((bf16[4,128,256]{2,1,0:T(8,128)(2,1)}), bf16[4,128,256]{2,1,0:T(8,128)(2,1)S(1)}, u32[]{:S(2)}, u32[]{:S(2)}) async-start(bf16[4,128,256]{2,1,0:T(8,128)(2,1)} %get-tuple-element.60), calls=%async_computation.1 | async-start | bytes 524288 | tf_op jit(solution)/shard_map/all_to_all | solution.py:86
  91.0 7.2 %copy-start.28 = (pred[4]{0:T(512)(128)(4,1)S(1)}, pred[4]{0:T(512)(128)(4,1)}, u32[]{:S(2)}) copy-start(pred[4]{0:T(512)(128)(4,1)} %copy-done.27) | copy-start | bytes 16
  97.4 11.5 %copy-start.26 = (pred[24]{0:T(512)(128)(4,1)S(1)}, pred[24]{0:T(512)(128)(4,1)}, u32[]{:S(2)}) copy-start(pred[24]{0:T(512)(128)(4,1)} %copy-done.25) | copy-start | bytes 76
  98.9 9.2 %all-to-all-start.5 = ((bf16[4,4,2048]{2,1,0:T(4,128)(2,1)}), bf16[4,4,2048]{2,1,0:T(4,128)(2,1)S(1)}, u32[]{:S(2)}, u32[]{:S(2)}) async-start(bf16[4,4,2048]{2,1,0:T(4,128)(2,1)} %copy.78), calls=%async_computation.5 | async-start | bytes 131072 | tf_op jit(solution)/shard_map/all_to_all | solution.py:113
where the time goes:
time: 111 us; the launch traced here: 110 us
  local copies, waits for them, and re-layouts  34.1 us (31%)
  starting transfers between devices  25 us (23%)
  waiting for transfers between devices  23.1 us (21%)
  other arithmetic  16.7 us (15%)
  matrix products  10.3 us (9%)
  between operations  1.18 us (1%)
    gather x5, local copies, waits for them, and re-layouts, rows_out(): picked = jnp.take(table, send_slot, axis=axis_pos, mode='clip')  7.08 us
    all_to_all x1, starting transfers between devices, on_device(): lax.all_to_all(rows_out(new_values, 1), 'dp', split_axis=0, concat_axis=0...  6.32 us
    all_to_all x1, waiting for transfers between devices, on_device(): lax.all_to_all(rows_out(key_cache, 0), 'dp', split_axis=0, concat_axis=0,...  5.83 us
    sub x1, matrix products, attend_rows(): exponent = jnp.exp(scores - highest)  5.19 us
    all_to_all x1, starting transfers between devices, on_device(): lax.all_to_all(rows_out(new_keys, 1), 'dp', split_axis=0, concat_axis=0,...  5.09 us
    all_to_all x1, waiting for transfers between devices, on_device(): lax.all_to_all(rows_out(queries, 1), 'dp', split_axis=0, concat_axis=0, t...  5.05 us
    all_to_all x1, waiting for transfers between devices, on_device(): lax.all_to_all(rows_out(value_cache, 0), 'dp', split_axis=0, concat_axis=...  4.99 us
    all_to_all x1, waiting for transfers between devices, on_device(): lax.all_to_all(jnp.transpose(going_back, (1, 0, 2)), 'dp', split_axis=0,...  4.67 us
  transfers between devices with their start and end apart: 6, of which 5 were waited for; matrix products, arithmetic and copies ran while one was open for 46% of the time, Pallas kernels for 0%

commit v1 on v0

v1 whole, which is shorter than its diff:
```python
import functools

import jax
import jax.numpy as jnp
from jax import lax
from jax.experimental import pallas as pl
from jax.experimental.pallas import tpu as pltpu
from jax.sharding import PartitionSpec as P

HEAD_DIM = 128
MESH = pl.DeviceIdType.MESH
masked_score = -1e30


def partner(me, n, i):
    if n % 2 or n < 4:
        return lax.rem(me + i + 1, n), lax.rem(me + n - i - 1, n)
    h = n // 2
    half = me // h
    pos = me % h
    if i < h:
        base = (1 - half) * h
        return base + (pos + i) % h, base + (pos + h - i) % h
    step = i - h + 1
    base = half * h
    return base + (pos + step) % h, base + (pos + h - step) % h


def slot_of_source(me, n, src):
    if n % 2 or n < 4:
        return jnp.clip(lax.rem(me - src + n, n) - 1, 0, n - 2)
    h = n // 2
    diff = (me % h + h - src % h) % h
    slot = jnp.where(me // h == src // h, h + diff - 1, diff)
    return jnp.clip(slot, 0, n - 2)


def kernel(
    n, rows, leave, land, steps, cap, width, qwidth,
    len_ref, mig_ref, cnt_ref, q_hbm, nk_hbm, nv_hbm, k_hbm, v_hbm,
    attn_hbm, lk_hbm, lv_hbm,
    q, nk, nv, k, v, nkf, nvf, qf, of, attn, sk, sv, rk, rv, lk, lv,
    in_sem, send_sem, recv_sem, out_sem,
):
    me = lax.axis_index("dp")
    kv_local = width // HEAD_DIM
    heads = qwidth // HEAD_DIM
    per = heads // kv_local
    block = heads * steps

    ins = []
    for i, (src, dst) in enumerate(((nk_hbm, nk), (k_hbm, k), (nv_hbm, nv), (v_hbm, v), (q_hbm, q))):
        copy = pltpu.make_async_copy(src, dst, in_sem.at[i])
        copy.start()
        ins.append(copy)

    barrier = pltpu.get_barrier_semaphore()
    for i in range(n - 1):
        pl.semaphore_signal(
            barrier, inc=1, device_id={"dp": partner(me, n, i)[0]}, device_id_type=MESH
        )

    def find_slot(peer):
        def body(j, carry):
            at = me * leave + j
            return jnp.where(mig_ref[at, 2] == peer, mig_ref[at, 0] - me * rows, carry)

        return jnp.clip(lax.fori_loop(0, leave, body, jnp.int32(0), unroll=leave <= 4), 0, rows - 1)

    slots = [find_slot(partner(me, n, i)[0]) for i in range(n - 1)]
    slot_lengths = [len_ref[me * rows + s] for s in slots]
    positions = lax.broadcasted_iota(jnp.int32, (cap, width), 0)

    def extend(cache, fresh, row, length):
        out = jnp.where(positions < length, cache[row].astype(jnp.float32), 0.0)
        for j in range(steps):
            out = jnp.where(positions == length + j, fresh[pl.ds(j * rows + row, 1), :], out)
        return out.astype(jnp.bfloat16)

    sends = [[], []]

    def push(which, cache, fresh, staged, landing):
        for i in range(n - 1):
            staged[i] = extend(cache, fresh, slots[i], slot_lengths[i])
            copy = pltpu.make_async_remote_copy(
                src_ref=staged.at[i],
                dst_ref=landing.at[i],
                send_sem=send_sem.at[which, i],
                recv_sem=recv_sem.at[which, i],
                device_id={"dp": partner(me, n, i)[0]},
                device_id_type=MESH,
            )
            copy.start()
            sends[which].append(copy)

    ins[0].wait()
    for j in range(steps):
        nkf[j * rows : (j + 1) * rows, :] = nk[j].astype(jnp.float32)
    ins[1].wait()
    pl.semaphore_wait(barrier, n - 1)
    push(0, k, nkf, sk, rk)
    ins[2].wait()
    for j in range(steps):
        nvf[j * rows : (j + 1) * rows, :] = nv[j].astype(jnp.float32)
    ins[3].wait()
    push(1, v, nvf, sv, rv)

    ins[4].wait()
    for s in range(steps):
        for h in range(heads):
            qf[pl.ds(h * steps + s, rows, stride=block), :] = q[
                s, :, h * HEAD_DIM : (h + 1) * HEAD_DIM
            ].astype(jnp.float32)

    span = per * steps
    at = lax.broadcasted_iota(jnp.int32, (span, cap), 1)
    step_of = lax.broadcasted_iota(jnp.int32, (span, cap), 0) % steps
    reach = at - step_of

    def attend(r, carry):
        length = len_ref[me * rows + r]
        ke = extend(k, nkf, r, length)
        ve = extend(v, nvf, r, length)
        for c in range(kv_local):
            cols = slice(c * HEAD_DIM, (c + 1) * HEAD_DIM)
            rowsl = pl.ds(pl.multiple_of(r * block, block) + c * span, span)
            qh = qf[rowsl, :].astype(jnp.bfloat16)
            sc = lax.dot_general(
                qh, ke[:, cols], (((1,), (1,)), ((), ())), preferred_element_type=jnp.float32
            ) * HEAD_DIM ** (-0.5)
            sc = jnp.where(reach <= length, sc, masked_score)
            e = jnp.exp(sc - jnp.max(sc, axis=-1, keepdims=True))
            w = (e / jnp.sum(e, axis=-1, keepdims=True)).astype(jnp.bfloat16)
            of[rowsl, :] = jnp.dot(w, ve[:, cols], preferred_element_type=jnp.float32)
        return carry

    lax.fori_loop(0, rows, attend, 0, unroll=2)
    for s in range(steps):
        for h in range(heads):
            attn[s, :, h * HEAD_DIM : (h + 1) * HEAD_DIM] = of[
                pl.ds(h * steps + s, rows, stride=block), :
            ].astype(jnp.bfloat16)
    out_attn = pltpu.make_async_copy(attn, attn_hbm, out_sem.at[0])
    out_attn.start()

    count = cnt_ref[me]

    def find_source(t):
        def body(m, carry):
            seen, src = carry
            hit = mig_ref[m, 2] == me
            src = jnp.where(hit & (seen == t), m // leave, src)
            return seen + hit.astype(jnp.int32), src

        seen, src = lax.fori_loop(
            0, n * leave, body, (jnp.int32(0), jnp.int32(0)), unroll=n * leave <= 8
        )
        return slot_of_source(me, n, src), (t < seen) & (t < count)

    outs = []
    picks = [find_source(t) for t in range(land)]
    for which, (landing, staged, out) in enumerate(((rk, lk, lk_hbm), (rv, lv, lv_hbm))):
        for copy in sends[which]:
            copy.wait_recv()
        for t, (slot, valid) in enumerate(picks):
            staged[t] = jnp.where(valid, landing[slot].astype(jnp.float32), 0.0).astype(jnp.bfloat16)
        copy = pltpu.make_async_copy(staged, out, out_sem.at[1 + which])
        copy.start()
        outs.append(copy)
    for group in sends:
        for copy in group:
            copy.wait_send()
    out_attn.wait()
    for copy in outs:
        copy.wait()


def on_device(
    queries, new_keys, new_values, key_cache, value_cache, lengths, migrations, receive_counts
):
    n = lax.axis_size("dp")
    rows, cap, width = key_cache.shape
    steps, _, qwidth = queries.shape
    leave = migrations.shape[0] // n
    land = leave + 1
    heads = qwidth // HEAD_DIM
    bf16, f32 = jnp.bfloat16, jnp.float32
    smem = pl.BlockSpec(memory_space=pltpu.SMEM)
    hbm = pl.BlockSpec(memory_space=pl.ANY)
    row_set = (cap, width)
    return pl.pallas_call(
        functools.partial(kernel, n, rows, leave, land, steps, cap, width, qwidth),
        out_shape=(
            jax.ShapeDtypeStruct(queries.shape, bf16),
            jax.ShapeDtypeStruct((land,) + row_set, bf16),
            jax.ShapeDtypeStruct((land,) + row_set, bf16),
        ),
        in_specs=[smem] * 3 + [hbm] * 5,
        out_specs=(hbm, hbm, hbm),
        scratch_shapes=[
            pltpu.VMEM(queries.shape, bf16),
            pltpu.VMEM(new_keys.shape, bf16),
            pltpu.VMEM(new_values.shape, bf16),
            pltpu.VMEM(key_cache.shape, bf16),
            pltpu.VMEM(value_cache.shape, bf16),
            pltpu.VMEM((steps * rows, width), f32),
            pltpu.VMEM((steps * rows, width), f32),
            pltpu.VMEM((rows * heads * steps, HEAD_DIM), f32),
            pltpu.VMEM((rows * heads * steps, HEAD_DIM), f32),
            pltpu.VMEM(queries.shape, bf16),
            pltpu.VMEM((n - 1,) + row_set, bf16),
            pltpu.VMEM((n - 1,) + row_set, bf16),
            pltpu.VMEM((n - 1,) + row_set, bf16),
            pltpu.VMEM((n - 1,) + row_set, bf16),
            pltpu.VMEM((land,) + row_set, bf16),
            pltpu.VMEM((land,) + row_set, bf16),
            pltpu.SemaphoreType.DMA((5,)),
            pltpu.SemaphoreType.DMA((2, n - 1)),
            pltpu.SemaphoreType.DMA((2, n - 1)),
            pltpu.SemaphoreType.DMA((3,)),
        ],
        compiler_params=pltpu.CompilerParams(
            collective_id=0, has_side_effects=True, vmem_limit_bytes=56 * 2**20
        ),
        name="migrate_attend",
    )(
        lengths, migrations, receive_counts, queries, new_keys, new_values, key_cache, value_cache
    )


def solution(mesh):
    placed = (
        P(None, ("groups", "dp"), "mp"),
        P(None, ("groups", "dp"), "mp"),
        P(None, ("groups", "dp"), "mp"),
        P(("groups", "dp"), None, "mp"),
        P(("groups", "dp"), None, "mp"),
        P("groups"),
        P("groups", None),
        P("groups"),
    )
    return jax.shard_map(
        on_device,
        mesh=mesh,
        in_specs=placed,
        out_specs=(
            P(None, ("groups", "dp"), "mp"),
            P(("groups", "dp"), None, "mp"),
            P(("groups", "dp"), None, "mp"),
        ),
        check_vma=False,
    )
```

time: 111 us -> 32.6 us (0.29)
  local copies, waits for them, and re-layouts: 34.1 us -> 6.35 us
  Pallas kernels: 0 us -> 25.4 us
  starting transfers between devices: 25 us -> 0 us
  waiting for transfers between devices: 23.1 us -> 0 us
  other arithmetic: 16.7 us -> 0 us
  matrix products: 10.3 us -> 0 us
    pallas_call x0 -> x1, Pallas kernels: none -> 25.4 us  [on_device(): pl.pallas_call(functools.partial(kernel, n, rows, leave, land, steps, cap...]
    all_to_all x6 -> x0, starting transfers between devices: 25 us -> none  [the longest x1 6.32 us: on_device(): lax.all_to_all(rows_out(new_values, 1), 'dp', split_axis=0, concat_axis=0...]
    gather x21 -> x0, local copies, waits for them, and re-layouts: 24.6 us -> none  [the longest x5 7.08 us: rows_out(): picked = jnp.take(table, send_slot, axis=axis_pos, mode='clip')]
    all_to_all x6 -> x0, waiting for transfers between devices: 23.1 us -> none  [the longest x1 5.83 us: on_device(): lax.all_to_all(rows_out(key_cache, 0), 'dp', split_axis=0, concat_axis=0,...]
    sub x1 -> x0, matrix products: 5.19 us -> none  [attend_rows(): exponent = jnp.exp(scores - highest)]
    dot_general x3 -> x0, matrix products: 5.07 us -> none  [the longest x2 4.21 us: attend_rows(): jnp.einsum('rkgsp,rpkd->srkgd', weights, value_view, preferred_element_ty...]
    unnamed x81 -> x4, local copies, waits for them, and re-layouts: 1.44 us -> 6.35 us
    eq x9 -> x0, other arithmetic: 3.54 us -> none  [the longest x7 3.53 us: extend_cache(): positions == limits + offset]
  transfers between devices with their start and end apart: 6 -> 0, of which waited for: 5 -> 0; matrix products, arithmetic and copies ran while one was open for 46% -> 0% of each run, Pallas kernels for 0% -> 0%
where the time goes in v1:
time: 32.6 us; the launch traced here: 32.4 us
  Pallas kernels  25.4 us (78%)
  local copies, waits for them, and re-layouts  6.35 us (19%)
  between operations  0.64 us (2%)
    pallas_call x1, Pallas kernels, on_device(): pl.pallas_call(functools.partial(kernel, n, rows, leave, land, steps, cap...  25.4 us
    unnamed x4, local copies, waits for them, and re-layouts  6.35 us

profile of v1, /device:TPU:0, one launch (start us, length us, event | category | flops | bytes accessed | tf_op | source)
XLA Modules:
  0.0 32.4 jit_solution(16708975304536889580)
XLA Ops:
  0.6 1.3 %copy.11.mig_ref = s32[8,3]{1,0:T(8,128)} copy(s32[8,3]{0,1:T(4,128)} %param.14) | data formatting | bytes 192 | tf_op args[6]
  2.0 25.4 %migrate_attend.1 = (bf16[4,24,2048]{2,1,0:T(8,128)(2,1)}, bf16[3,128,256]{2,1,0:T(8,128)(2,1)}, bf16[3,128,256]{2,1,0:T(8,128)(2,1)}) custom-call(s32[96]{0:T(128)} %len_ref.1, s32[8,3]{1,0:T(8,128)} %copy.11.mig_ref, s32[4]{0:T(128)} %cnt_ref.1, bf16[4,24,2048]{2,1,0:T(8,128)(2,1)} %q_hbm.1, bf16[4,24,256]{2,1,0:T(8,128)(2,1)} %nk_hbm.1, ...), custom_call_target="tpu_custom_call" | custom-call | tf_op jit(solution)/shard_map/migrate_attend/pallas_call | solution.py:191
  27.4 1.8 %copy.15 = bf16[4,24,2048]{2,1,0:T(8,128)(2,1)} copy(bf16[4,24,2048]{2,1,0:T(8,128)(2,1)} %get-tuple-element.6) | data formatting | bytes 786432
  29.1 1.6 %copy.16 = bf16[3,128,256]{2,1,0:T(8,128)(2,1)} copy(bf16[3,128,256]{2,1,0:T(8,128)(2,1)} %get-tuple-element.7) | data formatting | bytes 393216
  30.7 1.6 %copy.17 = bf16[3,128,256]{2,1,0:T(8,128)(2,1)} copy(bf16[3,128,256]{2,1,0:T(8,128)(2,1)} %get-tuple-element.8) | data formatting | bytes 393216

commit v2 on v1

--- a/solution.py
+++ b/solution.py
@@ -10,6 +10,8 @@
 HEAD_DIM = 128
 MESH = pl.DeviceIdType.MESH
 masked_score = -1e30
+LONGEST_STAYING = 32
+GROUP = 8
 
 
 def partner(me, n, i):
@@ -35,11 +37,21 @@
     return jnp.clip(slot, 0, n - 2)
 
 
+def slot_of_target(me, n, dest):
+    if n % 2 or n < 4:
+        return jnp.clip(lax.rem(dest - me + n, n) - 1, 0, n - 2)
+    h = n // 2
+    diff = (dest % h + h - me % h) % h
+    slot = jnp.where(me // h == dest // h, h + diff - 1, diff)
+    return jnp.clip(slot, 0, n - 2)
+
+
 def kernel(
     n, rows, leave, land, steps, cap, width, qwidth,
-    len_ref, mig_ref, cnt_ref, q_hbm, nk_hbm, nv_hbm, k_hbm, v_hbm,
+    len_hbm, mig_hbm, cnt_hbm, q_hbm, nk_hbm, nv_hbm, k_hbm, v_hbm,
     attn_hbm, lk_hbm, lv_hbm,
-    q, nk, nv, k, v, nkf, nvf, qf, of, attn, sk, sv, rk, rv, lk, lv,
+    len_ref, mig_ref, cnt_ref,
+    q, nk, nv, k, v, nkf, nvf, qf, of, ofl, attn, sk, sv, rk, rv, lk, lv,
     in_sem, send_sem, recv_sem, out_sem,
 ):
     me = lax.axis_index("dp")
@@ -47,9 +59,21 @@
     heads = qwidth // HEAD_DIM
     per = heads // kv_local
     block = heads * steps
+    window = min(cap, -(-(LONGEST_STAYING + steps) // 16) * 16)
 
     ins = []
-    for i, (src, dst) in enumerate(((nk_hbm, nk), (k_hbm, k), (nv_hbm, nv), (v_hbm, v), (q_hbm, q))):
+    for i, (src, dst) in enumerate(
+        (
+            (mig_hbm, mig_ref),
+            (len_hbm, len_ref),
+            (cnt_hbm, cnt_ref),
+            (nk_hbm, nk),
+            (k_hbm, k),
+            (nv_hbm, nv),
+            (v_hbm, v),
+            (q_hbm, q),
+        )
+    ):
         copy = pltpu.make_async_copy(src, dst, in_sem.at[i])
         copy.start()
         ins.append(copy)
@@ -59,20 +83,24 @@
         pl.semaphore_signal(
             barrier, inc=1, device_id={"dp": partner(me, n, i)[0]}, device_id_type=MESH
         )
+    for i in range(3):
+        ins[i].wait()
+
+    def own_slot(j):
+        return jnp.clip(mig_ref[0, me * leave + j] - me * rows, 0, rows - 1)
 
     def find_slot(peer):
         def body(j, carry):
-            at = me * leave + j
-            return jnp.where(mig_ref[at, 2] == peer, mig_ref[at, 0] - me * rows, carry)
-
-        return jnp.clip(lax.fori_loop(0, leave, body, jnp.int32(0), unroll=leave <= 4), 0, rows - 1)
+            return jnp.where(mig_ref[2, me * leave + j] == peer, own_slot(j), carry)
+
+        return lax.fori_loop(0, leave, body, jnp.int32(0), unroll=leave <= 4)
 
     slots = [find_slot(partner(me, n, i)[0]) for i in range(n - 1)]
     slot_lengths = [len_ref[me * rows + s] for s in slots]
-    positions = lax.broadcasted_iota(jnp.int32, (cap, width), 0)
-
-    def extend(cache, fresh, row, length):
-        out = jnp.where(positions < length, cache[row].astype(jnp.float32), 0.0)
+
+    def extend(cache, fresh, row, length, size):
+        positions = lax.broadcasted_iota(jnp.int32, (size, width), 0)
+        out = jnp.where(positions < length, cache[row, :size].astype(jnp.float32), 0.0)
         for j in range(steps):
             out = jnp.where(positions == length + j, fresh[pl.ds(j * rows + row, 1), :], out)
         return out.astype(jnp.bfloat16)
@@ -81,7 +109,7 @@
 
     def push(which, cache, fresh, staged, landing):
         for i in range(n - 1):
-            staged[i] = extend(cache, fresh, slots[i], slot_lengths[i])
+            staged[i] = extend(cache, fresh, slots[i], slot_lengths[i], cap)
             copy = pltpu.make_async_remote_copy(
                 src_ref=staged.at[i],
                 dst_ref=landing.at[i],
@@ -93,19 +121,19 @@
             copy.start()
             sends[which].append(copy)
 
-    ins[0].wait()
+    ins[3].wait()
     for j in range(steps):
         nkf[j * rows : (j + 1) * rows, :] = nk[j].astype(jnp.float32)
-    ins[1].wait()
+    ins[4].wait()
     pl.semaphore_wait(barrier, n - 1)
     push(0, k, nkf, sk, rk)
-    ins[2].wait()
+    ins[5].wait()
     for j in range(steps):
         nvf[j * rows : (j + 1) * rows, :] = nv[j].astype(jnp.float32)
-    ins[3].wait()
+    ins[6].wait()
     push(1, v, nvf, sv, rv)
 
-    ins[4].wait()
+    ins[7].wait()
     for s in range(steps):
         for h in range(heads):
             qf[pl.ds(h * steps + s, rows, stride=block), :] = q[
@@ -113,28 +141,73 @@
             ].astype(jnp.float32)
 
     span = per * steps
-    at = lax.broadcasted_iota(jnp.int32, (span, cap), 1)
-    step_of = lax.broadcasted_iota(jnp.int32, (span, cap), 0) % steps
-    reach = at - step_of
-
-    def attend(r, carry):
-        length = len_ref[me * rows + r]
-        ke = extend(k, nkf, r, length)
-        ve = extend(v, nvf, r, length)
-        for c in range(kv_local):
-            cols = slice(c * HEAD_DIM, (c + 1) * HEAD_DIM)
-            rowsl = pl.ds(pl.multiple_of(r * block, block) + c * span, span)
-            qh = qf[rowsl, :].astype(jnp.bfloat16)
-            sc = lax.dot_general(
-                qh, ke[:, cols], (((1,), (1,)), ((), ())), preferred_element_type=jnp.float32
+
+    def attend(entries, size):
+        reach = lax.broadcasted_iota(jnp.int32, (span, size), 1) - (
+            lax.broadcasted_iota(jnp.int32, (span, size), 0) % steps
+        )
+        pairs = [(e, c) for e in entries for c in range(kv_local)]
+        cols = [slice(c * HEAD_DIM, (c + 1) * HEAD_DIM) for c in range(kv_local)]
+        qs = [
+            qf[pl.ds(row * block + c * span, span), :].astype(jnp.bfloat16)
+            for (row, _, _, _), c in pairs
+        ]
+        scs = [
+            lax.dot_general(
+                qh, ke[:, cols[c]], (((1,), (1,)), ((), ())), preferred_element_type=jnp.float32
             ) * HEAD_DIM ** (-0.5)
-            sc = jnp.where(reach <= length, sc, masked_score)
-            e = jnp.exp(sc - jnp.max(sc, axis=-1, keepdims=True))
-            w = (e / jnp.sum(e, axis=-1, keepdims=True)).astype(jnp.bfloat16)
-            of[rowsl, :] = jnp.dot(w, ve[:, cols], preferred_element_type=jnp.float32)
+            for qh, ((_, _, ke, _), c) in zip(qs, pairs)
+        ]
+        scs = [
+            jnp.where(reach <= length, sc, masked_score)
+            for sc, ((_, length, _, _), _) in zip(scs, pairs)
+        ]
+        tops = [jnp.max(sc, axis=-1, keepdims=True) for sc in scs]
+        exps = [jnp.exp(sc - top) for sc, top in zip(scs, tops)]
+        sums = [jnp.sum(e, axis=-1, keepdims=True) for e in exps]
+        ws = [(e / total).astype(jnp.bfloat16) for e, total in zip(exps, sums)]
+        return [
+            jnp.dot(w, ve[:, cols[c]], preferred_element_type=jnp.float32)
+            for w, ((_, _, _, ve), c) in zip(ws, pairs)
+        ]
+
+    def attend_leaving(g, carry):
+        entries = []
+        for d in range(leave_group):
+            slot = own_slot(g * leave_group + d)
+            at = slot_of_target(me, n, mig_ref[2, me * leave + g * leave_group + d])
+            entries.append((slot, len_ref[me * rows + slot], sk[at], sv[at]))
+        parts = attend(entries, cap)
+        for x, part in enumerate(parts):
+            start = (g * leave_group + x // kv_local) * block + x % kv_local * span
+            ofl[pl.ds(pl.multiple_of(start, 8), span), :] = part
         return carry
 
-    lax.fori_loop(0, rows, attend, 0, unroll=2)
+    leave_group = 2 if leave % 2 == 0 else 1
+    lax.fori_loop(0, leave // leave_group, attend_leaving, 0)
+
+    def attend_rows(g, carry):
+        entries, redone = [], []
+        for d in range(group):
+            r = g * group + d
+            length = len_ref[me * rows + r]
+            at = jnp.int32(-1)
+            for j in range(leave):
+                at = jnp.where(own_slot(j) == r, j, at)
+            entries.append(
+                (r, length, extend(k, nkf, r, length, window), extend(v, nvf, r, length, window))
+            )
+            for c in range(kv_local):
+                start = jnp.maximum(at, 0) * block + c * span
+                redone.append((at >= 0, ofl[pl.ds(start, span), :]))
+        parts = attend(entries, window)
+        for x, (part, (again, other)) in enumerate(zip(parts, redone)):
+            start = (g * group + x // kv_local) * block + x % kv_local * span
+            of[pl.ds(pl.multiple_of(start, 8), span), :] = jnp.where(again, other, part)
+        return carry
+
+    group = GROUP if rows % GROUP == 0 else 1
+    lax.fori_loop(0, rows // group, attend_rows, 0)
     for s in range(steps):
         for h in range(heads):
             attn[s, :, h * HEAD_DIM : (h + 1) * HEAD_DIM] = of[
@@ -148,7 +221,7 @@
     def find_source(t):
         def body(m, carry):
             seen, src = carry
-            hit = mig_ref[m, 2] == me
+            hit = mig_ref[2, m] == me
             src = jnp.where(hit & (seen == t), m // leave, src)
             return seen + hit.astype(jnp.int32), src
 
@@ -175,6 +248,21 @@
         copy.wait()
 
 
+def hand_over(*refs):
+    count = (len(refs) - 2) // 3
+    given, result, held = refs[:count], refs[count : 2 * count], refs[2 * count : 3 * count]
+    in_sem, out_sem = refs[3 * count :]
+    ins = [pltpu.make_async_copy(given[i], held[i], in_sem.at[i]) for i in range(count)]
+    outs = [pltpu.make_async_copy(held[i], result[i], out_sem.at[i]) for i in range(count)]
+    for copy in ins:
+        copy.start()
+    for i in range(count):
+        ins[i].wait()
+        outs[i].start()
+    for copy in outs:
+        copy.wait()
+
+
 def on_device(
     queries, new_keys, new_values, key_cache, value_cache, lengths, migrations, receive_counts
 ):
@@ -185,19 +273,21 @@
     land = leave + 1
     heads = qwidth // HEAD_DIM
     bf16, f32 = jnp.bfloat16, jnp.float32
-    smem = pl.BlockSpec(memory_space=pltpu.SMEM)
     hbm = pl.BlockSpec(memory_space=pl.ANY)
     row_set = (cap, width)
-    return pl.pallas_call(
+    results = pl.pallas_call(
         functools.partial(kernel, n, rows, leave, land, steps, cap, width, qwidth),
         out_shape=(
             jax.ShapeDtypeStruct(queries.shape, bf16),
             jax.ShapeDtypeStruct((land,) + row_set, bf16),
             jax.ShapeDtypeStruct((land,) + row_set, bf16),
         ),
-        in_specs=[smem] * 3 + [hbm] * 5,
+        in_specs=[hbm] * 8,
         out_specs=(hbm, hbm, hbm),
         scratch_shapes=[
+            pltpu.SMEM(lengths.shape, jnp.int32),
+            pltpu.SMEM(migrations.shape[::-1], jnp.int32),
+            pltpu.SMEM(receive_counts.shape, jnp.int32),
             pltpu.VMEM(queries.shape, bf16),
             pltpu.VMEM(new_keys.shape, bf16),
             pltpu.VMEM(new_values.shape, bf16),
@@ -207,6 +297,7 @@
             pltpu.VMEM((steps * rows, width), f32),
             pltpu.VMEM((rows * heads * steps, HEAD_DIM), f32),
             pltpu.VMEM((rows * heads * steps, HEAD_DIM), f32),
+            pltpu.VMEM((leave * heads * steps, HEAD_DIM), f32),
             pltpu.VMEM(queries.shape, bf16),
             pltpu.VMEM((n - 1,) + row_set, bf16),
             pltpu.VMEM((n - 1,) + row_set, bf16),
@@ -214,7 +305,7 @@
             pltpu.VMEM((n - 1,) + row_set, bf16),
             pltpu.VMEM((land,) + row_set, bf16),
             pltpu.VMEM((land,) + row_set, bf16),
-            pltpu.SemaphoreType.DMA((5,)),
+            pltpu.SemaphoreType.DMA((8,)),
             pltpu.SemaphoreType.DMA((2, n - 1)),
             pltpu.SemaphoreType.DMA((2, n - 1)),
             pltpu.SemaphoreType.DMA((3,)),
@@ -224,8 +315,18 @@
         ),
         name="migrate_attend",
     )(
-        lengths, migrations, receive_counts, queries, new_keys, new_values, key_cache, value_cache
+        lengths, migrations.T, receive_counts, queries, new_keys, new_values, key_cache, value_cache
     )
+    return pl.pallas_call(
+        hand_over,
+        out_shape=tuple(jax.ShapeDtypeStruct(r.shape, r.dtype) for r in results),
+        in_specs=[hbm] * 3,
+        out_specs=(hbm,) * 3,
+        scratch_shapes=[pltpu.VMEM(r.shape, r.dtype) for r in results]
+        + [pltpu.SemaphoreType.DMA((3,))] * 2,
+        compiler_params=pltpu.CompilerParams(vmem_limit_bytes=56 * 2**20),
+        name="hand_over",
+    )(*results)
 
 
 def solution(mesh):

time: 32.6 us -> 20.4 us (0.63)
  local copies, waits for them, and re-layouts: 6.35 us -> 0 us
  Pallas kernels: 25.4 us -> 19.6 us
    pallas_call x1, Pallas kernels: 25.4 us -> 17.7 us  [on_device(): pl.pallas_call(functools.partial(kernel, n, rows, leave, land, steps, cap...]
    unnamed x4 -> x0, local copies, waits for them, and re-layouts: 6.35 us -> none
    pallas_call x0 -> x1, Pallas kernels: none -> 1.92 us  [on_device(): pl.pallas_call(hand_over, out_shape=tuple((jax.ShapeDtypeStruct(r.shape,...]
where the time goes in v2:
time: 20.4 us; the launch traced here: 20.3 us
  Pallas kernels  19.6 us (96%)
  between operations  0.64 us (3%)
    pallas_call x1, Pallas kernels, on_device(): pl.pallas_call(functools.partial(kernel, n, rows, leave, land, steps, cap...  17.7 us
    pallas_call x1, Pallas kernels, on_device(): pl.pallas_call(hand_over, out_shape=tuple((jax.ShapeDtypeStruct(r.shape,...  1.92 us

profile of v2, /device:TPU:0, one launch (start us, length us, event | category | flops | bytes accessed | tf_op | source)
XLA Modules:
  0.0 20.3 jit_solution(3204518284509894538)
XLA Ops:
  0.6 17.7 %migrate_attend.1 = (bf16[4,24,2048]{2,1,0:T(8,128)(2,1)}, bf16[3,128,256]{2,1,0:T(8,128)(2,1)}, bf16[3,128,256]{2,1,0:T(8,128)(2,1)}) custom-call(s32[96]{0:T(128)} %len_hbm.1, s32[3,8]{1,0:T(4,128)} %bitcast.1, s32[4]{0:T(128)} %cnt_hbm.1, bf16[4,24,2048]{2,1,0:T(8,128)(2,1)} %q_hbm.1, bf16[4,24,256]{2,1,0:T(8,128)(2,1)} %nk_hbm.1, ...), custom_call_target="tpu_custom_call" | custom-call | tf_op jit(solution)/shard_map/migrate_attend/pallas_call | solution.py:278
  18.3 1.9 %hand_over.1 = (bf16[4,24,2048]{2,1,0:T(8,128)(2,1)}, bf16[3,128,256]{2,1,0:T(8,128)(2,1)}, bf16[3,128,256]{2,1,0:T(8,128)(2,1)}) custom-call(bf16[4,24,2048]{2,1,0:T(8,128)(2,1)} %get-tuple-element.6.refs_0_, bf16[3,128,256]{2,1,0:T(8,128)(2,1)} %get-tuple-element.7.refs_1_, bf16[3,128,256]{2,1,0:T(8,128)(2,1)} %get-tuple-element.8.refs_2_), custom_call_target="tpu_custom_call" | custom-call | tf_op jit(solution)/shard_map/hand_over/pallas_call | solution.py:320

commit v3 on v2

--- a/solution.py
+++ b/solution.py
@@ -49,10 +49,10 @@
 def kernel(
     n, rows, leave, land, steps, cap, width, qwidth,
     len_hbm, mig_hbm, cnt_hbm, q_hbm, nk_hbm, nv_hbm, k_hbm, v_hbm,
-    attn_hbm, lk_hbm, lv_hbm,
+    attn, lk, lv,
     len_ref, mig_ref, cnt_ref,
-    q, nk, nv, k, v, nkf, nvf, qf, of, ofl, attn, sk, sv, rk, rv, lk, lv,
-    in_sem, send_sem, recv_sem, out_sem,
+    q, nk, nv, k, v, nkf, nvf, qf, of, ofl, sk, sv, rk, rv,
+    in_sem, send_sem, recv_sem,
 ):
     me = lax.axis_index("dp")
     kv_local = width // HEAD_DIM
@@ -75,7 +75,8 @@
         )
     ):
         copy = pltpu.make_async_copy(src, dst, in_sem.at[i])
-        copy.start()
+        if i < 5:
+            copy.start()
         ins.append(copy)
 
     barrier = pltpu.get_barrier_semaphore()
@@ -125,6 +126,8 @@
     for j in range(steps):
         nkf[j * rows : (j + 1) * rows, :] = nk[j].astype(jnp.float32)
     ins[4].wait()
+    for i in range(5, 8):
+        ins[i].start()
     pl.semaphore_wait(barrier, n - 1)
     push(0, k, nkf, sk, rk)
     ins[5].wait()
@@ -213,8 +216,6 @@
             attn[s, :, h * HEAD_DIM : (h + 1) * HEAD_DIM] = of[
                 pl.ds(h * steps + s, rows, stride=block), :
             ].astype(jnp.bfloat16)
-    out_attn = pltpu.make_async_copy(attn, attn_hbm, out_sem.at[0])
-    out_attn.start()
 
     count = cnt_ref[me]
 
@@ -230,36 +231,25 @@
         )
         return slot_of_source(me, n, src), (t < seen) & (t < count)
 
-    outs = []
     picks = [find_source(t) for t in range(land)]
-    for which, (landing, staged, out) in enumerate(((rk, lk, lk_hbm), (rv, lv, lv_hbm))):
+    for which, (landing, landed) in enumerate(((rk, lk), (rv, lv))):
         for copy in sends[which]:
             copy.wait_recv()
         for t, (slot, valid) in enumerate(picks):
-            staged[t] = jnp.where(valid, landing[slot].astype(jnp.float32), 0.0).astype(jnp.bfloat16)
-        copy = pltpu.make_async_copy(staged, out, out_sem.at[1 + which])
-        copy.start()
-        outs.append(copy)
+            landed[t] = jnp.where(valid, landing[slot].astype(jnp.float32), 0.0).astype(jnp.bfloat16)
     for group in sends:
         for copy in group:
             copy.wait_send()
-    out_attn.wait()
-    for copy in outs:
-        copy.wait()
 
 
 def hand_over(*refs):
-    count = (len(refs) - 2) // 3
-    given, result, held = refs[:count], refs[count : 2 * count], refs[2 * count : 3 * count]
-    in_sem, out_sem = refs[3 * count :]
-    ins = [pltpu.make_async_copy(given[i], held[i], in_sem.at[i]) for i in range(count)]
-    outs = [pltpu.make_async_copy(held[i], result[i], out_sem.at[i]) for i in range(count)]
-    for copy in ins:
+    count = len(refs) // 2
+    copies = [
+        pltpu.make_async_copy(refs[i], refs[count + i], refs[-1].at[i]) for i in range(count)
+    ]
+    for copy in copies:
         copy.start()
-    for i in range(count):
-        ins[i].wait()
-        outs[i].start()
-    for copy in outs:
+    for copy in copies:
         copy.wait()
 
 
@@ -274,16 +264,17 @@
     heads = qwidth // HEAD_DIM
     bf16, f32 = jnp.bfloat16, jnp.float32
     hbm = pl.BlockSpec(memory_space=pl.ANY)
+    vmem = pl.BlockSpec(memory_space=pltpu.VMEM)
     row_set = (cap, width)
     results = pl.pallas_call(
         functools.partial(kernel, n, rows, leave, land, steps, cap, width, qwidth),
         out_shape=(
-            jax.ShapeDtypeStruct(queries.shape, bf16),
-            jax.ShapeDtypeStruct((land,) + row_set, bf16),
-            jax.ShapeDtypeStruct((land,) + row_set, bf16),
+            pltpu.VMEM(queries.shape, bf16),
+            pltpu.VMEM((land,) + row_set, bf16),
+            pltpu.VMEM((land,) + row_set, bf16),
         ),
         in_specs=[hbm] * 8,
-        out_specs=(hbm, hbm, hbm),
+        out_specs=(vmem, vmem, vmem),
         scratch_shapes=[
             pltpu.SMEM(lengths.shape, jnp.int32),
             pltpu.SMEM(migrations.shape[::-1], jnp.int32),
@@ -298,20 +289,16 @@
             pltpu.VMEM((rows * heads * steps, HEAD_DIM), f32),
             pltpu.VMEM((rows * heads * steps, HEAD_DIM), f32),
             pltpu.VMEM((leave * heads * steps, HEAD_DIM), f32),
-            pltpu.VMEM(queries.shape, bf16),
             pltpu.VMEM((n - 1,) + row_set, bf16),
             pltpu.VMEM((n - 1,) + row_set, bf16),
             pltpu.VMEM((n - 1,) + row_set, bf16),
             pltpu.VMEM((n - 1,) + row_set, bf16),
-            pltpu.VMEM((land,) + row_set, bf16),
-            pltpu.VMEM((land,) + row_set, bf16),
             pltpu.SemaphoreType.DMA((8,)),
             pltpu.SemaphoreType.DMA((2, n - 1)),
             pltpu.SemaphoreType.DMA((2, n - 1)),
-            pltpu.SemaphoreType.DMA((3,)),
         ],
         compiler_params=pltpu.CompilerParams(
-            collective_id=0, has_side_effects=True, vmem_limit_bytes=56 * 2**20
+            collective_id=0, has_side_effects=True, vmem_limit_bytes=60 * 2**20
         ),
         name="migrate_attend",
     )(
@@ -320,11 +307,10 @@
     return pl.pallas_call(
         hand_over,
         out_shape=tuple(jax.ShapeDtypeStruct(r.shape, r.dtype) for r in results),
-        in_specs=[hbm] * 3,
+        in_specs=[vmem] * 3,
         out_specs=(hbm,) * 3,
-        scratch_shapes=[pltpu.VMEM(r.shape, r.dtype) for r in results]
-        + [pltpu.SemaphoreType.DMA((3,))] * 2,
-        compiler_params=pltpu.CompilerParams(vmem_limit_bytes=56 * 2**20),
+        scratch_shapes=[pltpu.SemaphoreType.DMA((3,))],
+        compiler_params=pltpu.CompilerParams(vmem_limit_bytes=32 * 2**20),
         name="hand_over",
     )(*results)
 

time: 20.4 us -> 18.7 us (0.917)
  Pallas kernels: 19.6 us -> 17.9 us
    pallas_call x1, Pallas kernels: 1.92 us -> 0.9 us  [on_device(): pl.pallas_call(hand_over, out_shape=tuple((jax.ShapeDtypeStruct(r.shape,...]
    pallas_call x1, Pallas kernels: 17.7 us -> 17 us  [on_device(): pl.pallas_call(functools.partial(kernel, n, rows, leave, land, steps, cap...]
where the time goes in v3:
time: 18.7 us; the launch traced here: 18.5 us
  Pallas kernels  17.9 us (96%)
  between operations  0.64 us (3%)
    pallas_call x1, Pallas kernels, on_device(): pl.pallas_call(functools.partial(kernel, n, rows, leave, land, steps, cap...  17 us
    pallas_call x1, Pallas kernels, on_device(): pl.pallas_call(hand_over, out_shape=tuple((jax.ShapeDtypeStruct(r.shape,...  0.9 us

profile of v3, /device:TPU:0, one launch (start us, length us, event | category | flops | bytes accessed | tf_op | source)
XLA Modules:
  0.0 18.5 jit_solution(6333808357050314497)
XLA Ops:
  0.6 17.0 %migrate_attend.1 = (bf16[4,24,2048]{2,1,0:T(8,128)(2,1)S(1)}, bf16[3,128,256]{2,1,0:T(8,128)(2,1)S(1)}, bf16[3,128,256]{2,1,0:T(8,128)(2,1)S(1)}) custom-call(s32[96]{0:T(128)} %len_hbm.1, s32[3,8]{1,0:T(4,128)} %bitcast.1, s32[4]{0:T(128)} %cnt_hbm.1, bf16[4,24,2048]{2,1,0:T(8,128)(2,1)} %q_hbm.1, bf16[4,24,256]{2,1,0:T(8,128)(2,1)} %nk_hbm.1, ...), custom_call_target="tpu_custom_call" | custom-call | tf_op jit(solution)/shard_map/migrate_attend/pallas_call | solution.py:269
  17.6 0.9 %hand_over.1 = (bf16[4,24,2048]{2,1,0:T(8,128)(2,1)}, bf16[3,128,256]{2,1,0:T(8,128)(2,1)}, bf16[3,128,256]{2,1,0:T(8,128)(2,1)}) custom-call(bf16[4,24,2048]{2,1,0:T(8,128)(2,1)S(1)} %get-tuple-element.6.refs_0_, bf16[3,128,256]{2,1,0:T(8,128)(2,1)S(1)} %get-tuple-element.7.refs_1_, bf16[3,128,256]{2,1,0:T(8,128)(2,1)S(1)} %get-tuple-element.8.refs_2_), custom_call_target="tpu_custom_call" | custom-call | tf_op jit(solution)/shard_map/hand_over/pallas_call | solution.py:307

commit v4 on v3

--- a/solution.py
+++ b/solution.py
@@ -52,7 +52,7 @@
     attn, lk, lv,
     len_ref, mig_ref, cnt_ref,
     q, nk, nv, k, v, nkf, nvf, qf, of, ofl, sk, sv, rk, rv,
-    in_sem, send_sem, recv_sem,
+    in_sem, send_sem, recv_sem, late_sem,
 ):
     me = lax.axis_index("dp")
     kv_local = width // HEAD_DIM
@@ -80,10 +80,17 @@
         ins.append(copy)
 
     barrier = pltpu.get_barrier_semaphore()
-    for i in range(n - 1):
-        pl.semaphore_signal(
-            barrier, inc=1, device_id={"dp": partner(me, n, i)[0]}, device_id_type=MESH
-        )
+    last = n - 1
+    h = n // 2
+    half, pos = me // h, me % h
+
+    @pl.when(me != last)
+    def _():
+        for i in range(n - 1):
+            pl.semaphore_signal(
+                barrier, inc=1, device_id={"dp": partner(me, n, i)[0]}, device_id_type=MESH
+            )
+
     for i in range(3):
         ins[i].wait()
 
@@ -96,7 +103,9 @@
 
         return lax.fori_loop(0, leave, body, jnp.int32(0), unroll=leave <= 4)
 
-    slots = [find_slot(partner(me, n, i)[0]) for i in range(n - 1)]
+    order = [((1 - half) * h + x, (x - pos + h) % h) for x in range(h)]
+    order += [(half * h + (pos + x) % h, h + x - 1) for x in range(1, h)]
+    slots = [find_slot(peer) for peer, _ in order]
     slot_lengths = [len_ref[me * rows + s] for s in slots]
 
     def extend(cache, fresh, row, length, size):
@@ -108,15 +117,16 @@
 
     sends = [[], []]
 
-    def push(which, cache, fresh, staged, landing):
-        for i in range(n - 1):
-            staged[i] = extend(cache, fresh, slots[i], slot_lengths[i], cap)
+    def push(which, cache, fresh, staged, landing, turns):
+        for x in turns:
+            peer, i = order[x]
+            staged[i] = extend(cache, fresh, slots[x], slot_lengths[x], cap)
             copy = pltpu.make_async_remote_copy(
                 src_ref=staged.at[i],
                 dst_ref=landing.at[i],
                 send_sem=send_sem.at[which, i],
                 recv_sem=recv_sem.at[which, i],
-                device_id={"dp": partner(me, n, i)[0]},
+                device_id={"dp": peer},
                 device_id_type=MESH,
             )
             copy.start()
@@ -128,13 +138,36 @@
     ins[4].wait()
     for i in range(5, 8):
         ins[i].start()
-    pl.semaphore_wait(barrier, n - 1)
-    push(0, k, nkf, sk, rk)
+    pl.semaphore_wait(barrier, jnp.where(me == last, n - 1, n - 2))
+
+    @pl.when(me == last)
+    def _():
+        for i in range(n - 1):
+            pl.semaphore_signal(
+                late_sem, inc=1, device_id={"dp": partner(me, n, i)[0]}, device_id_type=MESH
+            )
+
+    early, final, near = range(h - 1), range(h - 1, h), range(h, n - 1)
+    push(0, k, nkf, sk, rk, early)
     ins[5].wait()
     for j in range(steps):
         nvf[j * rows : (j + 1) * rows, :] = nv[j].astype(jnp.float32)
     ins[6].wait()
-    push(1, v, nvf, sv, rv)
+    push(1, v, nvf, sv, rv, early)
+
+    @pl.when(half == 0)
+    def _():
+        pl.semaphore_wait(late_sem, 1)
+
+    push(0, k, nkf, sk, rk, final)
+    push(1, v, nvf, sv, rv, final)
+
+    @pl.when((half == 1) & (me != last))
+    def _():
+        pl.semaphore_wait(late_sem, 1)
+
+    push(0, k, nkf, sk, rk, near)
+    push(1, v, nvf, sv, rv, near)
 
     ins[7].wait()
     for s in range(steps):
@@ -296,6 +329,7 @@
             pltpu.SemaphoreType.DMA((8,)),
             pltpu.SemaphoreType.DMA((2, n - 1)),
             pltpu.SemaphoreType.DMA((2, n - 1)),
+            pltpu.SemaphoreType.REGULAR,
         ],
         compiler_params=pltpu.CompilerParams(
             collective_id=0, has_side_effects=True, vmem_limit_bytes=60 * 2**20

time: 18.7 us -> 17.2 us (0.920)
  Pallas kernels: 17.9 us -> 16.4 us
    pallas_call x1, Pallas kernels: 17 us -> 15.5 us  [on_device(): pl.pallas_call(functools.partial(kernel, n, rows, leave, land, steps, cap...]
where the time goes in v4:
time: 17.2 us; the launch traced here: 17.1 us
  Pallas kernels  16.4 us (95%)
  between operations  0.64 us (4%)
    pallas_call x1, Pallas kernels, on_device(): pl.pallas_call(functools.partial(kernel, n, rows, leave, land, steps, cap...  15.5 us
    pallas_call x1, Pallas kernels, on_device(): pl.pallas_call(hand_over, out_shape=tuple((jax.ShapeDtypeStruct(r.shape,...  0.9 us

profile of v4, /device:TPU:0, one launch (start us, length us, event | category | flops | bytes accessed | tf_op | source)
XLA Modules:
  0.0 17.1 jit_solution(2386355597812860018)
XLA Ops:
  0.6 15.5 %migrate_attend.1 = (bf16[4,24,2048]{2,1,0:T(8,128)(2,1)S(1)}, bf16[3,128,256]{2,1,0:T(8,128)(2,1)S(1)}, bf16[3,128,256]{2,1,0:T(8,128)(2,1)S(1)}) custom-call(s32[96]{0:T(128)} %len_hbm.1, s32[3,8]{1,0:T(4,128)} %bitcast.1, s32[4]{0:T(128)} %cnt_hbm.1, bf16[4,24,2048]{2,1,0:T(8,128)(2,1)} %q_hbm.1, bf16[4,24,256]{2,1,0:T(8,128)(2,1)} %nk_hbm.1, ...), custom_call_target="tpu_custom_call" | custom-call | tf_op jit(solution)/shard_map/migrate_attend/pallas_call | solution.py:302
  16.2 0.9 %hand_over.1 = (bf16[4,24,2048]{2,1,0:T(8,128)(2,1)}, bf16[3,128,256]{2,1,0:T(8,128)(2,1)}, bf16[3,128,256]{2,1,0:T(8,128)(2,1)}) custom-call(bf16[4,24,2048]{2,1,0:T(8,128)(2,1)S(1)} %get-tuple-element.6.refs_0_, bf16[3,128,256]{2,1,0:T(8,128)(2,1)S(1)} %get-tuple-element.7.refs_1_, bf16[3,128,256]{2,1,0:T(8,128)(2,1)S(1)} %get-tuple-element.8.refs_2_), custom_call_target="tpu_custom_call" | custom-call | tf_op jit(solution)/shard_map/hand_over/pallas_call | solution.py:341
